TPU v7x, 32 devices: a whole 2x2x4 slice. The times are simulated.
32 devices in a mesh: dp: 16 (over z, y, core), seq: 2 (over x).
Axes of the slice: x: 2, y: 2, z: 4, core: 2. Of those that a mesh axis runs over, the one named last changes fastest.
Arguments:
- inputs: bfloat16 [16, 1024, 768], P('dp', 'seq'), may hold values from -6 to 6
- modality: int32 [16, 1024], P('dp'), may hold values from 0 to 2, never falling along the last dimension, each value on 1 to 512 neighbouring positions
- key_valid_mask: int32 [16, 1024], P('dp'), may hold values 0 or 1
- output_gradient: bfloat16 [16, 1024, 768], P('dp', 'seq'), may hold values from -6 to 6
- mats: float32 [768, 9216], P('dp'), may hold values from -2 to 2
- mats_momentum: float32 [768, 9216], P('dp')
- mats_average: float32 [768, 9216], P('dp'), may hold values from -2 to 2
- smalls: float32 [768, 15], P('dp'), may hold values from -2 to 2
- smalls_momentum: float32 [768, 15], P('dp')
- smalls_average: float32 [768, 15], P('dp'), may hold values from -2 to 2
Outputs:
- block_out: bfloat16 [16, 1024, 768], P('dp', 'seq')
- input_grad: bfloat16 [16, 1024, 768], P('dp', 'seq')
- mats_grad: float32 [768, 9216], P('dp')
- new_mats: float32 [768, 9216], P('dp')
- new_mats_momentum: float32 [768, 9216], P('dp')
- new_mats_average: float32 [768, 9216], P('dp')
- smalls_grad: float32 [768, 15], P('dp')
- out_bias_grad: float32 [768], P('dp')
- new_smalls: float32 [768, 15], P('dp')
- new_smalls_momentum: float32 [768, 15], P('dp')
- new_smalls_average: float32 [768, 15], P('dp')
Inputs may be any that keep to these rules, and one draw needn't show every extreme that they name: Along a document's positions the modality never falls; each of the three fills 1 to 512 positions, one of them exactly that many.
All inputs are finite; a program needn't handle non-finite values. No bound on the sum of `key_valid_mask` on one device may be relied on, other than what follows from the above.
Results may differ from a plain program's by a relative error of at most 0.019.
Values may be sent and summed in bfloat16 or wider, within the bound.
No kernel may reach another device: no remote copies, remote signals or barrier semaphores. Data moves between devices by JAX's collectives and lax.ppermute only.
A program may use at most 192 MiB of HBM per device.

v0:
```python
import math
import jax
import jax.numpy as jnp
from jax import lax
from jax.sharding import PartitionSpec as P

MODEL_WIDTH = 768
H = 12
HD = 64
FF = 3072
epsilon = 1e-06
momentum_rate = 0.9
decay_rate = 0.0001
average_rate = 0.75
base_rate = 0.03
masked_score = -1e30


def product(left, right):
    return jnp.dot(left, right, preferred_element_type=jnp.float32)


def product_tn(left, right):
    return lax.dot_general(
        left, right, (((0,), (0,)), ((), ())), preferred_element_type=jnp.float32
    )


def product_nt(left, right):
    return lax.dot_general(
        left, right, (((1,), (1,)), ((), ())), preferred_element_type=jnp.float32
    )


def normalize(rows, gain, shift):
    mean = jnp.mean(rows, axis=-1, keepdims=True)
    centred = rows - mean
    spread = jnp.mean(centred * centred, axis=-1, keepdims=True)
    return centred * lax.rsqrt(spread + epsilon) * gain + shift


def exact_gelu(values):
    return jax.nn.gelu(values, approximate=False)


def head_scores(query_heads, key_heads, live_doc):
    scores = (
        jnp.einsum("qhe,khe->hqk", query_heads, key_heads, preferred_element_type=jnp.float32)
        * 0.125
    )
    return jnp.where(live_doc[None, None, :] > 0, scores, masked_score)


def attention_forward_pass(item):
    query_doc, keys_doc, values_doc, live_doc = item
    query_heads = query_doc.reshape(query_doc.shape[0], H, HD)
    key_heads = keys_doc.reshape(keys_doc.shape[0], H, HD)
    value_heads = values_doc.reshape(values_doc.shape[0], H, HD)
    scores = head_scores(query_heads, key_heads, live_doc)
    top = jnp.max(scores, axis=-1, keepdims=True)
    expd = jnp.exp(scores - top)
    total = jnp.sum(expd, axis=-1, keepdims=True)
    prob = (expd / total).astype(jnp.bfloat16)
    attention_output = jnp.einsum(
        "hqk,khe->qhe", prob, value_heads, preferred_element_type=jnp.float32
    )
    return (attention_output.reshape(query_doc.shape[0], H * HD), (top + jnp.log(total))[..., 0])


def attention_backward_pass(item):
    query_doc, keys_doc, values_doc, live_doc, log_sum_normalizer, grad_doc = item
    element_count = query_doc.shape[0]
    length = keys_doc.shape[0]
    query_heads = query_doc.reshape(element_count, H, HD)
    key_heads = keys_doc.reshape(length, H, HD)
    value_heads = values_doc.reshape(length, H, HD)
    grad_heads = grad_doc.reshape(element_count, H, HD)
    scores = head_scores(query_heads, key_heads, live_doc)
    prob = jnp.exp(scores - log_sum_normalizer[..., None])
    grad_prob = jnp.einsum(
        "qhe,khe->hqk", grad_heads, value_heads, preferred_element_type=jnp.float32
    )
    grad_values = jnp.einsum(
        "hqk,qhe->khe", prob.astype(jnp.bfloat16), grad_heads, preferred_element_type=jnp.float32
    )
    inner = jnp.sum(prob * grad_prob, axis=-1, keepdims=True)
    grad_scores = (prob * (grad_prob - inner)).astype(jnp.bfloat16)
    grad_query = (
        jnp.einsum("hqk,khe->qhe", grad_scores, key_heads, preferred_element_type=jnp.float32)
        * 0.125
    )
    grad_keys = (
        jnp.einsum("hqk,qhe->khe", grad_scores, query_heads, preferred_element_type=jnp.float32)
        * 0.125
    )
    return (
        grad_query.reshape(element_count, H * HD),
        grad_keys.reshape(length, H * HD),
        grad_values.reshape(length, H * HD),
    )


def per_device(
    inputs,
    modality,
    key_valid_mask,
    output_gradient,
    mats,
    mats_momentum,
    mats_average,
    smalls,
    smalls_momentum,
    smalls_average,
):
    docs, local_len, width = inputs.shape
    seq_len = modality.shape[1]
    rows = docs * local_len
    low_mats = mats.astype(jnp.bfloat16)
    w_qkv, w_out, w_up, w_down, whole_smalls = (
        lax.all_gather(low_mats[:, 0 : 3 * MODEL_WIDTH], "dp", axis=0, tiled=True),
        lax.all_gather(low_mats[:, 3 * MODEL_WIDTH : 4 * MODEL_WIDTH], "dp", axis=0, tiled=True),
        lax.all_gather(
            low_mats[:, 4 * MODEL_WIDTH : 4 * MODEL_WIDTH + FF], "dp", axis=0, tiled=True
        ),
        lax.all_gather(low_mats[:, 4 * MODEL_WIDTH + FF :], "dp", axis=0, tiled=True),
        lax.all_gather(smalls.astype(jnp.bfloat16), "dp", axis=0, tiled=True),
    )
    params = whole_smalls.astype(jnp.float32)
    bias_qkv = jnp.concatenate([params[:, 0], jnp.zeros_like(params[:, 0]), params[:, 1]])
    bias_up = jnp.transpose(params[:, 8:12]).reshape(FF)
    embed = jnp.transpose(whole_smalls[:, 12:15])
    leading_key = (jnp.arange(seq_len) == 0).astype(jnp.int32)
    valid_positions = jnp.maximum(key_valid_mask, leading_key[None, :])
    local_start = lax.axis_index("seq") * local_len
    local_modality = lax.dynamic_slice_in_dim(modality, local_start, local_len, 1)
    onehot = (
        local_modality.reshape(rows)[:, None] == jnp.arange(3, dtype=jnp.int32)[None, :]
    ).astype(jnp.bfloat16)
    x_in = inputs.reshape(rows, width).astype(jnp.float32) + product(onehot, embed)
    x_low = x_in.astype(jnp.bfloat16)
    qkv = (product(x_low, w_qkv) + bias_qkv).astype(jnp.bfloat16)
    query_documents = qkv[:, 0:width].reshape(docs, local_len, width)
    keys_local = qkv[:, width : 2 * width].reshape(docs, local_len, width)
    values_local = qkv[:, 2 * width :].reshape(docs, local_len, width)
    every_key, every_value = (
        lax.all_gather(keys_local, "seq", axis=1, tiled=True),
        lax.all_gather(values_local, "seq", axis=1, tiled=True),
    )
    attention_output, log_sum_normalizer = lax.map(
        attention_forward_pass, (query_documents, every_key, every_value, valid_positions)
    )
    out_low = attention_output.reshape(rows, width).astype(jnp.bfloat16)
    mixed = product(out_low, w_out) + params[:, 2]
    first_in = x_in + mixed
    first = normalize(first_in, params[:, 4], params[:, 5])
    first_low = first.astype(jnp.bfloat16)
    up = product(first_low, w_up) + bias_up
    act_low = exact_gelu(up).astype(jnp.bfloat16)
    ffo = product_nt(act_low, w_down) + params[:, 3]
    second_in = first + ffo
    result = normalize(second_in, params[:, 6], params[:, 7])
    block_out = result.astype(jnp.bfloat16).reshape(docs, local_len, width)
    w_qkv, w_out, w_up, w_down = (
        lax.all_gather(low_mats[:, 0 : 3 * MODEL_WIDTH], "dp", axis=0, tiled=True),
        lax.all_gather(low_mats[:, 3 * MODEL_WIDTH : 4 * MODEL_WIDTH], "dp", axis=0, tiled=True),
        lax.all_gather(
            low_mats[:, 4 * MODEL_WIDTH : 4 * MODEL_WIDTH + FF], "dp", axis=0, tiled=True
        ),
        lax.all_gather(low_mats[:, 4 * MODEL_WIDTH + FF :], "dp", axis=0, tiled=True),
    )
    grad_rows = output_gradient.reshape(rows, width).astype(jnp.float32)
    second_out, second_pull = jax.vjp(normalize, second_in, params[:, 6], params[:, 7])
    grad_second, grad_gain2, grad_shift2 = second_pull(grad_rows)
    grad_ffo = grad_second.astype(jnp.bfloat16)
    grad_bias_down = jnp.sum(grad_ffo.astype(jnp.float32), axis=0)
    grad_w_down = product_tn(grad_ffo, act_low)
    grad_act = product(grad_ffo, w_down)
    gelu_out, gelu_pull = jax.vjp(exact_gelu, up)
    grad_up = gelu_pull(grad_act)[0].astype(jnp.bfloat16)
    grad_bias_up = jnp.sum(grad_up.astype(jnp.float32), axis=0)
    grad_w_up = product_tn(first_low, grad_up)
    grad_first = grad_second + product_nt(grad_up, w_up)
    first_out, first_pull = jax.vjp(normalize, first_in, params[:, 4], params[:, 5])
    grad_first_in, grad_gain1, grad_shift1 = first_pull(grad_first)
    grad_mixed = grad_first_in.astype(jnp.bfloat16)
    grad_bias_out = jnp.sum(grad_mixed.astype(jnp.float32), axis=0)
    grad_w_out = product_tn(out_low, grad_mixed)
    grad_out = product_nt(grad_mixed, w_out).astype(jnp.bfloat16)
    output_gradient_documents = grad_out.reshape(docs, local_len, width)
    grad_query, grad_keys_all, grad_values_all = lax.map(
        attention_backward_pass,
        (
            query_documents,
            every_key,
            every_value,
            valid_positions,
            log_sum_normalizer,
            output_gradient_documents,
        ),
    )
    grad_keys, grad_values = (
        lax.psum_scatter(
            grad_keys_all.astype(jnp.bfloat16), "seq", scatter_dimension=1, tiled=True
        ).astype(jnp.float32),
        lax.psum_scatter(
            grad_values_all.astype(jnp.bfloat16), "seq", scatter_dimension=1, tiled=True
        ).astype(jnp.float32),
    )
    grad_qkv = jnp.concatenate(
        [
            grad_query.reshape(rows, width).astype(jnp.bfloat16),
            grad_keys.reshape(rows, width).astype(jnp.bfloat16),
            grad_values.reshape(rows, width).astype(jnp.bfloat16),
        ],
        axis=1,
    )
    grad_bias_qkv = jnp.sum(grad_qkv.astype(jnp.float32), axis=0)
    grad_w_qkv = product_tn(x_low, grad_qkv)
    grad_x_in = grad_first_in + product_nt(grad_qkv, w_qkv)
    grad_embed = lax.dot_general(
        onehot.astype(jnp.float32),
        grad_x_in,
        (((0,), (0,)), ((), ())),
        precision=lax.Precision.HIGHEST,
        preferred_element_type=jnp.float32,
    )
    input_grad = grad_x_in.astype(jnp.bfloat16).reshape(docs, local_len, width)
    grad_columns = jnp.stack(
        [
            grad_bias_qkv[0:width],
            grad_bias_qkv[2 * width :],
            grad_bias_out,
            grad_bias_down,
            grad_gain1,
            grad_shift1,
            grad_gain2,
            grad_shift2,
        ],
        axis=1,
    )
    grad_smalls = jnp.concatenate(
        [
            grad_columns,
            jnp.transpose(grad_bias_up.reshape(FF // width, width)),
            jnp.transpose(grad_embed),
        ],
        axis=1,
    )
    qkv_shard, out_shard, up_shard, down_shard, small_shard = (
        lax.psum_scatter(
            grad_w_qkv.astype(jnp.bfloat16), "dp", scatter_dimension=0, tiled=True
        ).astype(jnp.float32),
        lax.psum_scatter(
            grad_w_out.astype(jnp.bfloat16), "dp", scatter_dimension=0, tiled=True
        ).astype(jnp.float32),
        lax.psum_scatter(
            grad_w_up.astype(jnp.bfloat16), "dp", scatter_dimension=0, tiled=True
        ).astype(jnp.float32),
        lax.psum_scatter(
            grad_w_down.astype(jnp.bfloat16), "dp", scatter_dimension=0, tiled=True
        ).astype(jnp.float32),
        lax.psum_scatter(
            grad_smalls.astype(jnp.bfloat16), "dp", scatter_dimension=0, tiled=True
        ).astype(jnp.float32),
    )
    mats_shard = jnp.concatenate([qkv_shard, out_shard, up_shard, down_shard], axis=1)
    mats_grad, smalls_grad = (
        lax.psum(mats_shard.astype(jnp.bfloat16), "seq").astype(jnp.float32),
        lax.psum(small_shard.astype(jnp.bfloat16), "seq").astype(jnp.float32),
    )
    out_bias_grad = smalls_grad[:, 2]
    total_tokens = rows * lax.axis_size("dp") * lax.axis_size("seq")
    rate = base_rate / math.sqrt(total_tokens)
    decayed = mats_grad + decay_rate * mats
    new_mats_momentum = momentum_rate * mats_momentum + decayed
    new_mats = mats - rate * (decayed + momentum_rate * new_mats_momentum)
    new_mats_average = average_rate * mats_average + (1.0 - average_rate) * new_mats
    new_smalls_momentum = momentum_rate * smalls_momentum + smalls_grad
    new_smalls = smalls - rate * (smalls_grad + momentum_rate * new_smalls_momentum)
    new_smalls_average = average_rate * smalls_average + (1.0 - average_rate) * new_smalls
    return (
        block_out,
        input_grad,
        mats_grad,
        new_mats,
        new_mats_momentum,
        new_mats_average,
        smalls_grad,
        out_bias_grad,
        new_smalls,
        new_smalls_momentum,
        new_smalls_average,
    )


def solution(mesh):
    placed = (
        P("dp", "seq", None),
        P("dp", None),
        P("dp", None),
        P("dp", "seq", None),
        P("dp", None),
        P("dp", None),
        P("dp", None),
        P("dp", None),
        P("dp", None),
        P("dp", None),
    )
    return jax.shard_map(
        per_device,
        mesh=mesh,
        in_specs=placed,
        out_specs=(
            P("dp", "seq", None),
            P("dp", "seq", None),
            P("dp", None),
            P("dp", None),
            P("dp", None),
            P("dp", None),
            P("dp", None),
            P("dp"),
            P("dp", None),
            P("dp", None),
            P("dp", None),
        ),
        check_vma=False,
    )
```

profile of v0, /device:TPU:0, one launch (start us, length us, event | category | flops | bytes accessed | tf_op | source)
XLA Modules:
  0.0 777.8 jit_solution(7473604885597649127)
XLA Ops:
  10.4 23.3 %all-gather.2 = bf16[16,48,15]{1,2,0:T(8,128)(2,1)S(1)} all-gather(bf16[1,48,15]{1,2,0:T(8,128)(2,1)S(1)} %convert_bitcast_fusion.1), channel_id=1, replica_groups=mesh['dp'=16,'seq'=2] {'dp'}, dimensions={0}, use_global_device_ids=true | all-gather | bytes 24480 | tf_op jit(solution)/shard_map/all_gather | solution.py:126
  34.9 25.7 %all-gather.10.cloned.1.call-done = bf16[768,2304]{1,0:T(8,128)(2,1)} async-done(((bf16[48,2304]{1,0:T(8,128)(2,1)}), bf16[768,2304]{1,0:T(8,128)(2,1)}) %all-gather.10.cloned.1.call-update) | async-done | bytes 3538960 | tf_op jit(solution)/shard_map/all_gather | solution.py:120
  69.5 22.8 %all-gather.20.cloned.1.call-done = bf16[1024,768]{1,0:T(8,128)(2,1)} async-done(((bf16[512,768]{1,0:T(8,128)(2,1)}), bf16[1024,768]{1,0:T(8,128)(2,1)}) %all-gather.20.cloned.1.call-update) | async-done | bytes 1572880 | tf_op jit(solution)/shard_map/all_gather | solution.py:146
  94.0 10.7 %fusion.6 = (f32[12,512]{1,0:T(8,128)S(1)}, f32[12,512,1024]{2,1,0:T(8,128)}) fusion(pred[1024]{0:T(1024)(128)(4,1)S(1)} %compare_reduce_fusion, bf16[512,12,64]{0,2,1:T(8,128)(2,1)S(1)} %bitcast.73, bf16[1024,12,64]{0,2,1:T(8,128)(2,1)S(1)} %bitcast.71), kind=kOutput, calls=%fused_computation.11 | convolution fusion | flops 824174592 | bytes 27550720 | tf_op jit(solution)/shard_map/while/body/eval_jaxpr/qhe,khe->hqk/dot_general | solution.py:48
  104.7 11.2 %fusion = f32[12,512]{1,0:T(8,128)S(1)} fusion(f32[12,512]{1,0:T(8,128)S(1)} %get-tuple-element.103, f32[12,512,1024]{2,1,0:T(8,128)} %get-tuple-element.104, pred[1024]{0:T(1024)(128)(4,1)S(1)} %compare_reduce_fusion), kind=kLoop, calls=%fused_computation.6 | loop fusion | flops 25159680 | bytes 25216000 | tf_op jit(solution)/shard_map/while/body/eval_jaxpr/reduce_sum | solution.py:62
  123.4 12.1 %fusion.21 = bf16[12,64,512]{2,1,0:T(8,128)(2,1)} fusion(bf16[1024,12,64]{0,2,1:T(8,128)(2,1)S(1)} %bitcast.76, f32[12,512]{1,0:T(8,128)S(1)} %fusion, f32[12,512]{1,0:T(8,128)S(1)} %get-tuple-element.103, f32[12,512,1024]{2,1,0:T(8,128)} %get-tuple-element.104, pred[1024]{0:T(1024)(128)(4,1)S(1)} %compare_reduce_fusion), kind=kOutput, calls=%fused_computation.65 | convolution fusion | flops 837156864 | bytes 27575296 | tf_op jit(solution)/shard_map/while/body/eval_jaxpr/hqk,khe->qhe/dot_general | solution.py:64
  135.5 27.3 %all-gather.12.cloned.1.call-done = bf16[768,768]{1,0:T(8,128)(2,1)} async-done(((bf16[48,768]{1,0:T(8,128)(2,1)}), bf16[768,768]{1,0:T(8,128)(2,1)}) %all-gather.12.cloned.1.call-update) | async-done | bytes 1179664 | tf_op jit(solution)/shard_map/all_gather | solution.py:121
  166.0 51.8 %all-gather.14.cloned.1.call-done = bf16[768,3072]{1,0:T(8,128)(2,1)} async-done(((bf16[48,3072]{1,0:T(8,128)(2,1)}), bf16[768,3072]{1,0:T(8,128)(2,1)}) %all-gather.14.cloned.1.call-update) | async-done | bytes 4718608 | tf_op jit(solution)/shard_map/all_gather | solution.py:122
  217.8 19.8 %multiply_convert_fusion.1 = (bf16[512,3072]{1,0:T(8,128)(2,1)}, f32[512,3072]{1,0:T(8,128)}, f32[512,3072]{1,0:T(8,128)}) fusion(f32[3072]{0:T(1024)S(1)} %add.163, bf16[768,3072]{1,0:T(8,128)(2,1)} %all-gather.14.cloned.1.call-done, f32[512,768]{1,0:T(8,128)S(1)} %get-tuple-element.106, f32[768]{0:T(1024)S(1)} %get-tuple-element.70, ...), kind=kOutput, calls=%fused_computation.15 | convolution fusion | flops 2521694208 | bytes 22042624 | tf_op jit(solution)/shard_map/dot_general | solution.py:20
  237.6 34.9 %all-gather.16.cloned.1.call-done = bf16[768,3072]{1,0:T(8,128)(2,1)} async-done(((bf16[48,3072]{1,0:T(8,128)(2,1)}), bf16[768,3072]{1,0:T(8,128)(2,1)}) %all-gather.16.cloned.1.call-update) | async-done | bytes 4718608 | tf_op jit(solution)/shard_map/all_gather | solution.py:125
  272.5 6.6 fusion.50
  283.9 7.0 fusion.40
  300.2 12.6 %fusion.16 = bf16[12,64,1024]{2,1,0:T(8,128)(2,1)} fusion(bf16[512,12,64]{0,2,1:T(8,128)(2,1)S(1)} %bitcast.81, f32[12,512]{1,0:T(8,128)S(1)} %log_add_fusion, f32[12,512,1024]{2,1,0:T(8,128)} %get-tuple-element.104, pred[1024]{0:T(1024)(128)(4,1)S(1)} %compare_reduce_fusion), kind=kOutput, calls=%fused_computation.46 | convolution fusion | flops 831258624 | bytes 27550720 | tf_op jit(solution)/shard_map/while/body/eval_jaxpr/hqk,qhe->khe/dot_general | solution.py:83
  312.9 20.8 %multiply_reduce_fusion = (f32[12,512]{1,0:T(8,128)S(1)}, f32[12,512,1024]{2,1,0:T(8,128)}) fusion(f32[12,512]{1,0:T(8,128)S(1)} %log_add_fusion, f32[12,512,1024]{2,1,0:T(8,128)} %get-tuple-element.104, pred[1024]{0:T(1024)(128)(4,1)S(1)} %compare_reduce_fusion, bf16[512,12,64]{0,2,1:T(8,128)(2,1)S(1)} %bitcast.82, bf16[1024,12,64]{0,2,1:T(8,128)(2,1)S(1)} %bitcast.77), kind=kOutput, calls=%fused_computation.1 | convolution fusion | flops 836757504 | bytes 52741120 | tf_op jit(solution)/shard_map/while/body/eval_jaxpr/qhe,khe->hqk/dot_general | solution.py:80
  333.7 16.9 %multiply_convert_fusion = bf16[12,512,1024]{2,1,0:T(8,128)(2,1)S(1)} fusion(f32[12,512,1024]{2,1,0:T(8,128)} %get-tuple-element.112, f32[12,512]{1,0:T(8,128)S(1)} %get-tuple-element.111, f32[12,512]{1,0:T(8,128)S(1)} %log_add_fusion, f32[12,512,1024]{2,1,0:T(8,128)} %get-tuple-element.104, pred[1024]{0:T(1024)(128)(4,1)S(1)} %compare_reduce_fusion), kind=kLoop, calls=%fused_computation | loop fusion | flops 37748736 | bytes 62964736 | tf_op jit(solution)/shard_map/while/body/eval_jaxpr/convert_element_type | solution.py:87
  358.9 6.8 convolution_convert_fusion.1
  366.9 6.3 convolution_convert_fusion
  374.5 8.6 %multiply_convert_fusion.3 = bf16[12,64,512]{2,1,0:T(8,128)(2,1)S(1)} fusion(bf16[1024,12,64]{0,2,1:T(8,128)(2,1)S(1)} %bitcast.72, bf16[12,512,1024]{2,1,0:T(8,128)(2,1)} %copy-done.2), kind=kOutput, calls=%fused_computation.51 | convolution fusion | flops 806092800 | bytes 14942208 | tf_op jit(solution)/shard_map/while/body/eval_jaxpr/hqk,khe->qhe/dot_general | solution.py:89
  398.1 44.1 %reduce-scatter.16.cloned.1.call-done = bf16[48,768]{1,0:T(8,128)(2,1)} async-done(((bf16[768,768]{1,0:T(8,128)(2,1)}), bf16[48,768]{1,0:T(8,128)(2,1)}) %reduce-scatter.16.cloned.1.call-update) | async-done | bytes 73744 | tf_op jit(solution)/shard_map/reduce_scatter | solution.py:253
  442.3 78.3 %reduce-scatter.18.cloned.1.call-done = bf16[48,3072]{1,0:T(8,128)(2,1)} async-done(((bf16[768,3072]{1,0:T(8,128)(2,1)}), bf16[48,3072]{1,0:T(8,128)(2,1)}) %reduce-scatter.18.cloned.1.call-update) | async-done | bytes 294928 | tf_op jit(solution)/shard_map/reduce_scatter | solution.py:256
  520.5 79.0 %reduce-scatter.20.cloned.1.call-done = bf16[48,3072]{1,0:T(8,128)(2,1)} async-done(((bf16[768,3072]{1,0:T(8,128)(2,1)}), bf16[48,3072]{1,0:T(8,128)(2,1)}) %reduce-scatter.20.cloned.1.call-update) | async-done | bytes 294928 | tf_op jit(solution)/shard_map/reduce_scatter | solution.py:259
  599.5 70.9 %reduce-scatter.14.cloned.1.call-done = bf16[48,2304]{1,0:T(8,128)(2,1)} async-done(((bf16[768,2304]{1,0:T(8,128)(2,1)}), bf16[48,2304]{1,0:T(8,128)(2,1)}) %reduce-scatter.14.cloned.1.call-update) | async-done | bytes 221200 | tf_op jit(solution)/shard_map/reduce_scatter | solution.py:250
  673.5 53.5 %reduce-scatter.22.cloned.1.call-done = bf16[48,15]{1,0:T(8,128)(2,1)} async-done(((bf16[768,15]{1,0:T(8,128)(2,1)}), bf16[48,15]{1,0:T(8,128)(2,1)}) %reduce-scatter.22.cloned.1.call-update) | async-done | bytes 1456
  733.9 31.4 %all-reduce.2.cloned.1.call-done = bf16[48,9216]{1,0:T(8,128)(2,1)} async-done(((bf16[48,9216]{1,0:T(8,128)(2,1)}), bf16[48,9216]{1,0:T(8,128)(2,1)}) %all-reduce.2.cloned.1.call-update) | async-done | bytes 884752 | tf_op jit(solution)/shard_map/psum | solution.py:268
  (167 shorter events, 80.7 us)
Async XLA Ops:
  7.2 26.7 %copy-start = (s32[1,1024]{1,0:T(1,128)S(1)}, s32[1,1024]{1,0:T(1,128)}, u32[]{:S(2)}) copy-start(s32[1,1024]{1,0:T(1,128)} %param.11) | copy-start | bytes 12292
  7.2 27.3 %copy-start.16 = (bf16[1,512,768]{2,1,0:T(8,128)(2,1)S(1)}, bf16[1,512,768]{2,1,0:T(8,128)(2,1)}, u32[]{:S(2)}) copy-start(bf16[1,512,768]{2,1,0:T(8,128)(2,1)} %param.10) | copy-start | bytes 2359300
  7.2 53.4 %all-gather.10.cloned.1.call-start = ((), (), s32[]{:S(2)}) async-start(), calls=%async_computation.7 | async-start | bytes 3760128 | tf_op jit(solution)/shard_map/all_gather | solution.py:120
  9.6 82.7 %all-gather.20.cloned.1.call-start = ((), (), s32[]{:S(2)}) async-start(), calls=%async_computation.19 | async-start | bytes 2359296 | tf_op jit(solution)/shard_map/all_gather | solution.py:146
  65.9 55.7 %all-gather.18.cloned.1.call-start = ((), (), s32[]{:S(2)}) async-start(), calls=%async_computation.18 | async-start | bytes 2359296 | tf_op jit(solution)/shard_map/all_gather | solution.py:147
  66.7 96.1 %all-gather.12.cloned.1.call-start = ((), (), s32[]{:S(2)}) async-start(), calls=%async_computation.8 | async-start | bytes 1253376 | tf_op jit(solution)/shard_map/all_gather | solution.py:121
  67.4 150.4 %all-gather.14.cloned.1.call-start = ((), (), s32[]{:S(2)}) async-start(), calls=%async_computation.9 | async-start | bytes 5013504 | tf_op jit(solution)/shard_map/all_gather | solution.py:122
  68.3 204.2 %all-gather.16.cloned.1.call-start = ((), (), s32[]{:S(2)}) async-start(), calls=%async_computation.10 | async-start | bytes 5013504 | tf_op jit(solution)/shard_map/all_gather | solution.py:125
  68.9 314.3 %reduce-scatter.12.cloned.1.call-start = ((), (), s32[]{:S(2)}) async-start(), calls=%async_computation.12 | async-start | bytes 2359296 | tf_op jit(solution)/shard_map/reduce_scatter | solution.py:205
  69.4 35.2 %copy-start.5 = (bf16[512,768]{0,1:T(8,128)(2,1)}, bf16[512,768]{0,1:T(8,128)(2,1)S(1)}, u32[]{:S(2)}) copy-start(bf16[512,768]{0,1:T(8,128)(2,1)S(1)} %copy.36) | copy-start | bytes 2359300
  165.7 72.0 %copy-start.11 = (f32[512,768]{1,0:T(8,128)}, f32[512,768]{1,0:T(8,128)S(1)}, u32[]{:S(2)}) copy-start(f32[512,768]{1,0:T(8,128)S(1)} %get-tuple-element.106) | copy-start | bytes 4718596
  312.9 70.3 %reduce-scatter.10.cloned.1.call-start = ((), (), s32[]{:S(2)}) async-start(), calls=%async_computation.11 | async-start | bytes 2359296 | tf_op jit(solution)/shard_map/reduce_scatter | solution.py:202
  355.7 86.6 %reduce-scatter.16.cloned.1.call-start = ((), (), s32[]{:S(2)}) async-start(), calls=%async_computation.14 | async-start | bytes 1253376 | tf_op jit(solution)/shard_map/reduce_scatter | solution.py:253
  358.8 161.7 %reduce-scatter.18.cloned.1.call-start = ((), (), s32[]{:S(2)}) async-start(), calls=%async_computation.15 | async-start | bytes 5013504 | tf_op jit(solution)/shard_map/reduce_scatter | solution.py:256
  365.8 233.8 %reduce-scatter.20.cloned.1.call-start = ((), (), s32[]{:S(2)}) async-start(), calls=%async_computation.16 | async-start | bytes 5013504 | tf_op jit(solution)/shard_map/reduce_scatter | solution.py:259
  373.2 297.3 %reduce-scatter.14.cloned.1.call-start = ((), (), s32[]{:S(2)}) async-start(), calls=%async_computation.13 | async-start | bytes 3760128 | tf_op jit(solution)/shard_map/reduce_scatter | solution.py:250
  389.1 337.9 %reduce-scatter.22.cloned.1.call-start = ((), (), s32[]{:S(2)}) async-start(), calls=%async_computation.20 | async-start | bytes 208896
  396.4 336.4 %copy-start.21 = (f32[48,15]{0,1:T(8,128)S(1)}, f32[48,15]{0,1:T(8,128)}, u32[]{:S(2)}) copy-start(f32[48,15]{0,1:T(8,128)} %param.17) | copy-start | bytes 8644
  396.4 336.4 %copy-start.24 = (f32[48,15]{0,1:T(8,128)S(1)}, f32[48,15]{0,1:T(8,128)}, u32[]{:S(2)}) copy-start(f32[48,15]{0,1:T(8,128)} %param.19) | copy-start | bytes 8644
  396.4 336.4 %copy-start.25 = (f32[48,15]{0,1:T(8,128)S(1)}, f32[48,15]{0,1:T(8,128)}, u32[]{:S(2)}) copy-start(f32[48,15]{0,1:T(8,128)} %param.18) | copy-start | bytes 8644
  396.4 368.9 %copy-start.7 = (f32[48,9216]{1,0:T(8,128)S(1)}, f32[48,9216]{1,0:T(8,128)}, u32[]{:S(2)}) copy-start(f32[48,9216]{1,0:T(8,128)} %param.14) | copy-start | bytes 5308420
  398.1 367.2 %all-reduce.2.cloned.1.call-start = ((), (), s32[]{:S(2)}) async-start(), calls=%async_computation.17 | async-start | bytes 1769472 | tf_op jit(solution)/shard_map/psum | solution.py:268
  733.4 37.7 %copy-start.26 = (f32[48,15]{0,1:T(8,128)}, f32[48,15]{0,1:T(8,128)S(1)}, u32[]{:S(2)}) copy-start(f32[48,15]{0,1:T(8,128)S(1)} %get-tuple-element.78) | copy-start | bytes 8644
  733.4 37.7 %copy-start.1 = (s32[1,1024]{1,0:T(1,128)S(1)}, s32[1,1024]{1,0:T(1,128)}, u32[]{:S(2)}) copy-start(s32[1,1024]{1,0:T(1,128)} %param.11) | copy-start | bytes 12292
  (24 other events, 144.2 us)
Sparse Core Ops, SparseCore 0:
  10.9 49.6 all-gather.9
  66.0 26.1 all-gather.19
  94.4 27.2 all-gather.17
  124.4 38.3 all-gather.11
  165.4 52.3 all-gather.13
  220.5 51.9 all-gather.15
  313.0 24.5 reduce-scatter.11
  355.8 24.6 reduce-scatter.9
  384.1 58.1 reduce-scatter.15
  446.0 74.5 reduce-scatter.17
  524.9 74.5 reduce-scatter.19
  603.3 67.1 reduce-scatter.13
  674.5 52.4 reduce-scatter.21
  729.8 35.4 all-reduce.1
where the time goes:
time: 781 us; the launch traced here: 778 us
  waiting for transfers between devices  527 us (67%)
  matrix products  142 us (18%)
  other arithmetic  46.1 us (6%)
  blocking collectives  28.3 us (4%)
  local copies, waits for them, and re-layouts  18.8 us (2%)
  between operations  14.7 us (2%)
    reduce_scatter x1, waiting for transfers between devices, per_device(): lax.psum_scatter(grad_w_down.astype(jnp.bfloat16), 'dp', scatter_dimensio...  79 us
    reduce_scatter x1, waiting for transfers between devices, per_device(): lax.psum_scatter(grad_w_up.astype(jnp.bfloat16), 'dp', scatter_dimension=...  78.3 us
    reduce_scatter x1, waiting for transfers between devices, per_device(): lax.psum_scatter(grad_w_qkv.astype(jnp.bfloat16), 'dp', scatter_dimension...  70.9 us
    unnamed x15, waiting for transfers between devices  54.9 us
    all_gather x1, waiting for transfers between devices, per_device(): lax.all_gather(low_mats[:, 4 * MODEL_WIDTH:4 * MODEL_WIDTH + FF], 'dp', a...  51.8 us
    reduce_scatter x1, waiting for transfers between devices, per_device(): lax.psum_scatter(grad_w_out.astype(jnp.bfloat16), 'dp', scatter_dimension...  44.1 us
    all_gather x1, waiting for transfers between devices, per_device(): lax.all_gather(low_mats[:, 4 * MODEL_WIDTH + FF:], 'dp', axis=0, tiled=True)  34.9 us
    dot_general x5, matrix products, product(): return jnp.dot(left, right, preferred_element_type=jnp.float32)  34.2 us
  transfers between devices with their start and end apart: 14, of which 12 were waited for; matrix products, arithmetic and copies ran while one was open for 19% of the time, Pallas kernels for 0%

commit v1 on v0

--- a/solution.py
+++ b/solution.py
@@ -14,6 +14,18 @@
 average_rate = 0.75
 base_rate = 0.03
 masked_score = -1e30
+
+
+def doubled_up(value, axis, dim):
+    ways, here, lap = (lax.axis_size(axis), lax.axis_index(axis), value.shape[dim])
+    line, have = (value, 1)
+    while have < ways:
+        line = jnp.concatenate(
+            [line, lax.ppermute(line, axis, [(d, (d - have) % ways) for d in range(ways)])],
+            axis=dim,
+        )
+        have = 2 * have
+    return jnp.roll(line, here * lap, axis=dim)
 
 
 def product(left, right):
@@ -119,9 +131,7 @@
     w_qkv, w_out, w_up, w_down, whole_smalls = (
         lax.all_gather(low_mats[:, 0 : 3 * MODEL_WIDTH], "dp", axis=0, tiled=True),
         lax.all_gather(low_mats[:, 3 * MODEL_WIDTH : 4 * MODEL_WIDTH], "dp", axis=0, tiled=True),
-        lax.all_gather(
-            low_mats[:, 4 * MODEL_WIDTH : 4 * MODEL_WIDTH + FF], "dp", axis=0, tiled=True
-        ),
+        doubled_up(low_mats[:, 4 * MODEL_WIDTH : 4 * MODEL_WIDTH + FF], "dp", 0),
         lax.all_gather(low_mats[:, 4 * MODEL_WIDTH + FF :], "dp", axis=0, tiled=True),
         lax.all_gather(smalls.astype(jnp.bfloat16), "dp", axis=0, tiled=True),
     )

time: 781 us -> 825 us (1.056)
  local copies, waits for them, and re-layouts: 18.8 us -> 33.8 us
  waiting for transfers between devices: 527 us -> 539 us
  starting transfers between devices: 0.92 us -> 11.5 us
    ppermute x0 -> x4, waiting for transfers between devices: none -> 133 us  [doubled_up(): lax.ppermute(line, axis, [(d, (d - have) % ways) for d in range(ways)])]
    all_gather x1, waiting for transfers between devices: 34.9 us -> 0.02 us  [per_device(): lax.all_gather(low_mats[:, 4 * MODEL_WIDTH + FF:], 'dp', axis=0, tiled=True)]
    all_gather x1, waiting for transfers between devices: 51.8 us -> 18.7 us  [per_device(): lax.all_gather(low_mats[:, 4 * MODEL_WIDTH:4 * MODEL_WIDTH + FF], 'dp', a...]
    all_gather x1, waiting for transfers between devices: 27.3 us -> 0.01 us  [per_device(): lax.all_gather(low_mats[:, 3 * MODEL_WIDTH:4 * MODEL_WIDTH], 'dp', axis=0...]
    all_gather x1, waiting for transfers between devices: 22.8 us -> 0.02 us  [per_device(): lax.all_gather(keys_local, 'seq', axis=1, tiled=True)]
    ppermute x0 -> x4, starting transfers between devices: none -> 10.6 us  [doubled_up(): lax.ppermute(line, axis, [(d, (d - have) % ways) for d in range(ways)])]
    unnamed x71 -> x88, local copies, waits for them, and re-layouts: 9.46 us -> 19.4 us
  transfers between devices with their start and end apart: 14 -> 18, of which waited for: 12 -> 10; matrix products, arithmetic and copies ran while one was open for 19% -> 23% of each run, Pallas kernels for 0% -> 0%
where the time goes in v1:
time: 825 us; the launch traced here: 821 us
  waiting for transfers between devices  539 us (65%)
  matrix products  148 us (18%)
  other arithmetic  48.3 us (6%)
  local copies, waits for them, and re-layouts  33.8 us (4%)
  blocking collectives  25 us (3%)
  between operations  14.8 us (2%)
  starting transfers between devices  11.5 us (1%)
    ppermute x4, waiting for transfers between devices, doubled_up(): lax.ppermute(line, axis, [(d, (d - have) % ways) for d in range(ways)])  133 us
    reduce_scatter x1, waiting for transfers between devices, per_device(): lax.psum_scatter(grad_w_down.astype(jnp.bfloat16), 'dp', scatter_dimensio...  78.9 us
    reduce_scatter x1, waiting for transfers between devices, per_device(): lax.psum_scatter(grad_w_up.astype(jnp.bfloat16), 'dp', scatter_dimension=...  78.3 us
    reduce_scatter x1, waiting for transfers between devices, per_device(): lax.psum_scatter(grad_w_qkv.astype(jnp.bfloat16), 'dp', scatter_dimension...  70.9 us
    unnamed x15, waiting for transfers between devices  54.2 us
    reduce_scatter x1, waiting for transfers between devices, per_device(): lax.psum_scatter(grad_w_out.astype(jnp.bfloat16), 'dp', scatter_dimension...  44.1 us
    dot_general x5, matrix products, product(): return jnp.dot(left, right, preferred_element_type=jnp.float32)  36 us
    psum x1, waiting for transfers between devices, per_device(): lax.psum(mats_shard.astype(jnp.bfloat16), 'seq').astype(jnp.float32)  31.4 us
  transfers between devices with their start and end apart: 18, of which 10 were waited for; matrix products, arithmetic and copies ran while one was open for 23% of the time, Pallas kernels for 0%

profile of v1, /device:TPU:0, one launch (start us, length us, event | category | flops | bytes accessed | tf_op | source)
XLA Modules:
  0.0 820.9 jit_solution(6704853497668655015)
XLA Ops:
  15.9 20.1 %all-gather.2 = bf16[16,48,15]{1,2,0:T(8,128)(2,1)S(1)} all-gather(bf16[1,48,15]{1,2,0:T(8,128)(2,1)S(1)} %convert_bitcast_fusion.1), channel_id=1, replica_groups=mesh['dp'=16,'seq'=2] {'dp'}, dimensions={0}, use_global_device_ids=true | all-gather | bytes 24480 | tf_op jit(solution)/shard_map/all_gather | solution.py:136
  38.6 30.2 %all-gather.10.cloned.1.call-done = bf16[768,2304]{1,0:T(8,128)(2,1)} async-done(((bf16[48,2304]{1,0:T(8,128)(2,1)}), bf16[768,2304]{1,0:T(8,128)(2,1)}) %all-gather.10.cloned.1.call-update) | async-done | bytes 3538960 | tf_op jit(solution)/shard_map/all_gather | solution.py:132
  79.7 25.9 %collective-permute-done.2 = bf16[192,3072]{1,0:T(8,128)(2,1)S(1)} collective-permute-done((bf16[192,3072]{1,0:T(8,128)(2,1)}, bf16[192,3072]{1,0:T(8,128)(2,1)S(1)}, u32[]{:S(2)}, u32[]{:S(2)}) %collective-permute-start.2) | collective-permute-done | bytes 1179680 | tf_op jit(solution)/shard_map/ppermute | solution.py:24
  112.0 106.7 %collective-permute-done.3 = bf16[384,3072]{1,0:T(8,128)(2,1)} collective-permute-done((bf16[384,3072]{1,0:T(8,128)(2,1)}, bf16[384,3072]{1,0:T(8,128)(2,1)}, u32[]{:S(2)}, u32[]{:S(2)}) %collective-permute-start.3) | collective-permute-done | bytes 2359328 | tf_op jit(solution)/shard_map/ppermute | solution.py:24
  232.0 10.2 %fusion.6 = (f32[12,512]{1,0:T(8,128)S(1)}, f32[12,512,1024]{2,1,0:T(8,128)}) fusion(pred[1024]{0:T(1024)(128)(4,1)S(1)} %compare_reduce_fusion, bf16[512,12,64]{0,2,1:T(8,128)(2,1)S(1)} %bitcast.72, bf16[1024,12,64]{0,2,1:T(8,128)(2,1)S(1)} %bitcast.70), kind=kOutput, calls=%fused_computation.11 | convolution fusion | flops 824174592 | bytes 27550720 | tf_op jit(solution)/shard_map/while/body/eval_jaxpr/qhe,khe->hqk/dot_general | solution.py:60
  242.2 11.5 %fusion = f32[12,512]{1,0:T(8,128)S(1)} fusion(f32[12,512]{1,0:T(8,128)S(1)} %get-tuple-element.105, f32[12,512,1024]{2,1,0:T(8,128)} %get-tuple-element.106, pred[1024]{0:T(1024)(128)(4,1)S(1)} %compare_reduce_fusion), kind=kLoop, calls=%fused_computation.6 | loop fusion | flops 25159680 | bytes 25216000 | tf_op jit(solution)/shard_map/while/body/eval_jaxpr/reduce_sum | solution.py:74
  255.5 12.3 %fusion.23 = bf16[12,64,512]{2,1,0:T(8,128)(2,1)} fusion(bf16[1024,12,64]{0,2,1:T(8,128)(2,1)S(1)} %bitcast.75, f32[12,512]{1,0:T(8,128)S(1)} %fusion, f32[12,512]{1,0:T(8,128)S(1)} %get-tuple-element.105, f32[12,512,1024]{2,1,0:T(8,128)} %get-tuple-element.106, pred[1024]{0:T(1024)(128)(4,1)S(1)} %compare_reduce_fusion), kind=kOutput, calls=%fused_computation.68 | convolution fusion | flops 837156864 | bytes 27575296 | tf_op jit(solution)/shard_map/while/body/eval_jaxpr/hqk,khe->qhe/dot_general | solution.py:76
  271.4 21.4 %multiply_convert_fusion.1 = (bf16[512,3072]{1,0:T(8,128)(2,1)}, f32[512,3072]{1,0:T(8,128)}, f32[512,3072]{1,0:T(8,128)}) fusion(f32[3072]{0:T(1024)S(1)} %add.175, bf16[1536,3072]{1,0:T(8,128)(2,1)} %constant_dynamic-update-slice_fusion, s32[]{:T(128)S(6)} %select_n.26, f32[512,768]{1,0:T(8,128)S(1)} %get-tuple-element.108, f32[768]{0:T(1024)S(1)} %copy-done.31, ...), kind=kOutput, calls=%fused_computation.15 | convolution fusion | flops 2521694208 | bytes 22042628 | tf_op jit(solution)/shard_map/dot_general | solution.py:32
  292.9 6.7 fusion.53
  305.3 6.1 fusion.42
  311.5 18.7 %all-gather.16.cloned.1.call-done = bf16[768,3072]{1,0:T(8,128)(2,1)} async-done(((bf16[48,3072]{1,0:T(8,128)(2,1)}), bf16[768,3072]{1,0:T(8,128)(2,1)}) %all-gather.16.cloned.1.call-update) | async-done | bytes 4718608 | tf_op jit(solution)/shard_map/all_gather | solution.py:176
  330.1 7.4 multiply_reduce_fusion.1
  343.5 12.6 %fusion.18 = bf16[12,64,1024]{2,1,0:T(8,128)(2,1)} fusion(bf16[512,12,64]{0,2,1:T(8,128)(2,1)S(1)} %bitcast.80, f32[12,512]{1,0:T(8,128)S(1)} %log_add_fusion, f32[12,512,1024]{2,1,0:T(8,128)} %get-tuple-element.106, pred[1024]{0:T(1024)(128)(4,1)S(1)} %compare_reduce_fusion), kind=kOutput, calls=%fused_computation.49 | convolution fusion | flops 831258624 | bytes 27550720 | tf_op jit(solution)/shard_map/while/body/eval_jaxpr/hqk,qhe->khe/dot_general | solution.py:95
  356.2 20.8 %multiply_reduce_fusion = (f32[12,512]{1,0:T(8,128)S(1)}, f32[12,512,1024]{2,1,0:T(8,128)}) fusion(f32[12,512]{1,0:T(8,128)S(1)} %log_add_fusion, f32[12,512,1024]{2,1,0:T(8,128)} %get-tuple-element.106, pred[1024]{0:T(1024)(128)(4,1)S(1)} %compare_reduce_fusion, bf16[512,12,64]{0,2,1:T(8,128)(2,1)S(1)} %bitcast.81, bf16[1024,12,64]{0,2,1:T(8,128)(2,1)S(1)} %bitcast.76), kind=kOutput, calls=%fused_computation.1 | convolution fusion | flops 836757504 | bytes 52741120 | tf_op jit(solution)/shard_map/while/body/eval_jaxpr/qhe,khe->hqk/dot_general | solution.py:92
  377.0 16.9 %multiply_convert_fusion = bf16[12,512,1024]{2,1,0:T(8,128)(2,1)S(1)} fusion(f32[12,512,1024]{2,1,0:T(8,128)} %get-tuple-element.114, f32[12,512]{1,0:T(8,128)S(1)} %get-tuple-element.113, f32[12,512]{1,0:T(8,128)S(1)} %log_add_fusion, f32[12,512,1024]{2,1,0:T(8,128)} %get-tuple-element.106, pred[1024]{0:T(1024)(128)(4,1)S(1)} %compare_reduce_fusion), kind=kLoop, calls=%fused_computation | loop fusion | flops 37748736 | bytes 62964736 | tf_op jit(solution)/shard_map/while/body/eval_jaxpr/convert_element_type | solution.py:99
  402.2 6.9 convolution_convert_fusion.1
  410.2 6.3 convolution_convert_fusion
  417.9 8.6 %multiply_convert_fusion.3 = bf16[12,64,512]{2,1,0:T(8,128)(2,1)S(1)} fusion(bf16[1024,12,64]{0,2,1:T(8,128)(2,1)S(1)} %bitcast.71, bf16[12,512,1024]{2,1,0:T(8,128)(2,1)} %copy-done.2), kind=kOutput, calls=%fused_computation.54 | convolution fusion | flops 806092800 | bytes 14942208 | tf_op jit(solution)/shard_map/while/body/eval_jaxpr/hqk,khe->qhe/dot_general | solution.py:101
  441.5 44.1 %reduce-scatter.16.cloned.1.call-done = bf16[48,768]{1,0:T(8,128)(2,1)} async-done(((bf16[768,768]{1,0:T(8,128)(2,1)}), bf16[48,768]{1,0:T(8,128)(2,1)}) %reduce-scatter.16.cloned.1.call-update) | async-done | bytes 73744 | tf_op jit(solution)/shard_map/reduce_scatter | solution.py:263
  485.6 78.3 %reduce-scatter.18.cloned.1.call-done = bf16[48,3072]{1,0:T(8,128)(2,1)} async-done(((bf16[768,3072]{1,0:T(8,128)(2,1)}), bf16[48,3072]{1,0:T(8,128)(2,1)}) %reduce-scatter.18.cloned.1.call-update) | async-done | bytes 294928 | tf_op jit(solution)/shard_map/reduce_scatter | solution.py:266
  563.9 78.9 %reduce-scatter.20.cloned.1.call-done = bf16[48,3072]{1,0:T(8,128)(2,1)} async-done(((bf16[768,3072]{1,0:T(8,128)(2,1)}), bf16[48,3072]{1,0:T(8,128)(2,1)}) %reduce-scatter.20.cloned.1.call-update) | async-done | bytes 294928 | tf_op jit(solution)/shard_map/reduce_scatter | solution.py:269
  642.8 70.9 %reduce-scatter.14.cloned.1.call-done = bf16[48,2304]{1,0:T(8,128)(2,1)} async-done(((bf16[768,2304]{1,0:T(8,128)(2,1)}), bf16[48,2304]{1,0:T(8,128)(2,1)}) %reduce-scatter.14.cloned.1.call-update) | async-done | bytes 221200 | tf_op jit(solution)/shard_map/reduce_scatter | solution.py:260
  716.7 53.4 %reduce-scatter.22.cloned.1.call-done = bf16[48,15]{1,0:T(8,128)(2,1)} async-done(((bf16[768,15]{1,0:T(8,128)(2,1)}), bf16[48,15]{1,0:T(8,128)(2,1)}) %reduce-scatter.22.cloned.1.call-update) | async-done | bytes 1456
  777.0 31.4 %all-reduce.2.cloned.1.call-done = bf16[48,9216]{1,0:T(8,128)(2,1)} async-done(((bf16[48,9216]{1,0:T(8,128)(2,1)}), bf16[48,9216]{1,0:T(8,128)(2,1)}) %all-reduce.2.cloned.1.call-update) | async-done | bytes 884752 | tf_op jit(solution)/shard_map/psum | solution.py:278
  (196 shorter events, 99.9 us)
Async XLA Ops:
  7.2 61.6 %all-gather.10.cloned.1.call-start = ((), (), s32[]{:S(2)}) async-start(), calls=%async_computation.7 | async-start | bytes 3760128 | tf_op jit(solution)/shard_map/all_gather | solution.py:132
  9.6 220.4 %all-gather.20.cloned.1.call-start = ((), (), s32[]{:S(2)}) async-start(), calls=%async_computation.19 | async-start | bytes 2359296 | tf_op jit(solution)/shard_map/all_gather | solution.py:156
  10.5 95.1 %copy-start.7 = (bf16[48,3072]{1,0:T(8,128)(2,1)}, bf16[48,3072]{1,0:T(8,128)(2,1)S(1)}, u32[]{:S(2)}) copy-start(bf16[48,3072]{1,0:T(8,128)(2,1)S(1)} %get-tuple-element.101) | copy-start | bytes 884740
  10.5 28.0 %collective-permute-start = (bf16[48,3072]{1,0:T(8,128)(2,1)S(1)}, bf16[48,3072]{1,0:T(8,128)(2,1)S(1)}, u32[]{:S(2)}, u32[]{:S(2)}) collective-permute-start(bf16[48,3072]{1,0:T(8,128)(2,1)S(1)} %get-tuple-element.101), channel_id=1, source_target_pairs={{0,30},{2,0},{4,2},{6,4},{8,6},{10,8},{12,10},{14,12},{16,14},{18,... | collective-permute-start | bytes 884744 | tf_op jit(solution)/shard_map/ppermute | solution.py:24
  38.5 36.3 %collective-permute-start.1 = (bf16[96,3072]{1,0:T(8,128)(2,1)S(1)}, bf16[96,3072]{1,0:T(8,128)(2,1)S(1)}, u32[]{:S(2)}, u32[]{:S(2)}) collective-permute-start(bf16[96,3072]{1,0:T(8,128)(2,1)S(1)} %pad_maximum_fusion.4), channel_id=1, source_target_pairs={{0,28},{2,30},{4,0},{6,2},{8,4},{10,6},{12,8},{14,10},{16,12},{18,... | collective-permute-start | bytes 1769480 | tf_op jit(solution)/shard_map/ppermute | solution.py:24
  74.8 179.0 %all-gather.18.cloned.1.call-start = ((), (), s32[]{:S(2)}) async-start(), calls=%async_computation.18 | async-start | bytes 2359296 | tf_op jit(solution)/shard_map/all_gather | solution.py:157
  75.9 29.6 %collective-permute-start.2 = (bf16[192,3072]{1,0:T(8,128)(2,1)}, bf16[192,3072]{1,0:T(8,128)(2,1)S(1)}, u32[]{:S(2)}, u32[]{:S(2)}) collective-permute-start(bf16[192,3072]{1,0:T(8,128)(2,1)} %pad_maximum_fusion.2), channel_id=1, source_target_pairs={{0,24},{2,26},{4,28},{6,30},{8,0},{10,2},{12,4},{14,6},{16,8},{18,... | collective-permute-start | bytes 3538952 | tf_op jit(solution)/shard_map/ppermute | solution.py:24
  79.6 188.2 %all-gather.12.cloned.1.call-start = ((), (), s32[]{:S(2)}) async-start(), calls=%async_computation.8 | async-start | bytes 1253376 | tf_op jit(solution)/shard_map/all_gather | solution.py:133
  107.1 111.6 %collective-permute-start.3 = (bf16[384,3072]{1,0:T(8,128)(2,1)}, bf16[384,3072]{1,0:T(8,128)(2,1)}, u32[]{:S(2)}, u32[]{:S(2)}) collective-permute-start(bf16[384,3072]{1,0:T(8,128)(2,1)} %pad_maximum_fusion), channel_id=1, source_target_pairs={{0,16},{2,18},{4,20},{6,22},{8,24},{10,26},{12,28},{14,30},{16,0},... | collective-permute-start | bytes 7077896 | tf_op jit(solution)/shard_map/ppermute | solution.py:24
  109.2 183.6 %all-gather.14.cloned.1.call-start = ((), (), s32[]{:S(2)}) async-start(), calls=%async_computation.9 | async-start | bytes 5013504 | tf_op jit(solution)/shard_map/all_gather | solution.py:135
  112.0 111.7 %copy-start.34 = (s32[1,1024]{1,0:T(1,128)S(1)}, s32[1,1024]{1,0:T(1,128)}, u32[]{:S(2)}) copy-start(s32[1,1024]{1,0:T(1,128)} %param.12) | copy-start | bytes 12292
  222.9 107.3 %all-gather.16.cloned.1.call-start = ((), (), s32[]{:S(2)}) async-start(), calls=%async_computation.10 | async-start | bytes 5013504 | tf_op jit(solution)/shard_map/all_gather | solution.py:176
  223.4 203.1 %reduce-scatter.12.cloned.1.call-start = ((), (), s32[]{:S(2)}) async-start(), calls=%async_computation.12 | async-start | bytes 2359296 | tf_op jit(solution)/shard_map/reduce_scatter | solution.py:215
  356.2 70.3 %reduce-scatter.10.cloned.1.call-start = ((), (), s32[]{:S(2)}) async-start(), calls=%async_computation.11 | async-start | bytes 2359296 | tf_op jit(solution)/shard_map/reduce_scatter | solution.py:212
  399.0 86.6 %reduce-scatter.16.cloned.1.call-start = ((), (), s32[]{:S(2)}) async-start(), calls=%async_computation.14 | async-start | bytes 1253376 | tf_op jit(solution)/shard_map/reduce_scatter | solution.py:263
  402.2 161.7 %reduce-scatter.18.cloned.1.call-start = ((), (), s32[]{:S(2)}) async-start(), calls=%async_computation.15 | async-start | bytes 5013504 | tf_op jit(solution)/shard_map/reduce_scatter | solution.py:266
  409.1 233.7 %reduce-scatter.20.cloned.1.call-start = ((), (), s32[]{:S(2)}) async-start(), calls=%async_computation.16 | async-start | bytes 5013504 | tf_op jit(solution)/shard_map/reduce_scatter | solution.py:269
  416.5 297.1 %reduce-scatter.14.cloned.1.call-start = ((), (), s32[]{:S(2)}) async-start(), calls=%async_computation.13 | async-start | bytes 3760128 | tf_op jit(solution)/shard_map/reduce_scatter | solution.py:260
  432.5 337.7 %reduce-scatter.22.cloned.1.call-start = ((), (), s32[]{:S(2)}) async-start(), calls=%async_computation.20 | async-start | bytes 208896
  439.7 336.2 %copy-start.25 = (f32[48,15]{0,1:T(8,128)S(1)}, f32[48,15]{0,1:T(8,128)}, u32[]{:S(2)}) copy-start(f32[48,15]{0,1:T(8,128)} %param.17) | copy-start | bytes 8644
  439.7 336.1 %copy-start.28 = (f32[48,15]{0,1:T(8,128)S(1)}, f32[48,15]{0,1:T(8,128)}, u32[]{:S(2)}) copy-start(f32[48,15]{0,1:T(8,128)} %param.19) | copy-start | bytes 8644
  439.7 336.1 %copy-start.29 = (f32[48,15]{0,1:T(8,128)S(1)}, f32[48,15]{0,1:T(8,128)}, u32[]{:S(2)}) copy-start(f32[48,15]{0,1:T(8,128)} %param.18) | copy-start | bytes 8644
  439.8 368.7 %copy-start.8 = (f32[48,9216]{1,0:T(8,128)S(1)}, f32[48,9216]{1,0:T(8,128)}, u32[]{:S(2)}) copy-start(f32[48,9216]{1,0:T(8,128)} %param.14) | copy-start | bytes 5308420
  441.4 367.0 %all-reduce.2.cloned.1.call-start = ((), (), s32[]{:S(2)}) async-start(), calls=%async_computation.17 | async-start | bytes 1769472 | tf_op jit(solution)/shard_map/psum | solution.py:278
  (33 other events, 346.6 us)
Sparse Core Ops, SparseCore 0:
  10.9 57.8 all-gather.9
  74.9 28.3 all-gather.19
  105.4 27.2 all-gather.17
  135.4 84.7 all-gather.11
  223.0 52.9 all-gather.13
  278.2 51.9 all-gather.15
  356.3 24.6 reduce-scatter.11
  399.1 24.6 reduce-scatter.9
  427.4 58.1 reduce-scatter.15
  489.3 74.5 reduce-scatter.17
  568.2 74.5 reduce-scatter.19
  646.5 67.0 reduce-scatter.13
  717.7 52.4 reduce-scatter.21
  772.9 35.4 all-reduce.1
